TPU v7x, 32 devices: a whole 2x2x4 slice. The times are simulated.
32 devices in a mesh: seq: 8 (over z, y), tp: 4 (over x, core).
Axes of the slice: x: 2, y: 2, z: 4, core: 2. Of those that a mesh axis runs over, the one named last changes fastest.
Arguments:
- tier_source_concatenated: bfloat16 [1024, 2048], P('seq', 'tp'), may hold values from -6 to 6
- prompt_sizes_ordered: int32 [4], replicated, may hold values from 1 to 512, 1024 in all
- tier_standardize_scale: float32 [2048], replicated, may hold values from 0.1 to 1.9
- tier_standardize_offset: float32 [2048], replicated, may hold values from -3 to 3
- previous_item_mixers: float32 [5, 2048], replicated, may hold values from 0 to 1
- mapping_matrices_pile: bfloat16 [4, 2048, 2048], P(None, None, 'tp'), may hold values from -0.125 to 0.125
- fading_narrow_left: bfloat16 [2048, 64], replicated, may hold values from -0.125 to 0.125
- fading_narrow_right: bfloat16 [64, 2048], P(None, 'tp'), may hold values from -0.75 to 0.75
- feature_fading_baseline: float32 [2048], P('tp'), may hold values from 5e-05 to 0.04
- diagonal_boost_coefficient: float32 [2048], P('tp'), may hold values from -4 to 4
- cluster_standardize_scale: float32 [2048], P('tp'), may hold values from 0.1 to 1.9
- cluster_standardize_offset: float32 [2048], P('tp'), may hold values from -3 to 3
- emitted_mapping_matrix: bfloat16 [2048, 2048], P('tp'), may hold values from -0.125 to 0.125
Outputs:
- hidden_out: bfloat16 [1024, 2048], P('seq', 'tp')
Inputs may be any that keep to these rules, and one draw needn't show every extreme that they name: `prompt_sizes_ordered`: the prompt lengths sum to 1024, and the longest is exactly 512.
All inputs are finite; a program needn't handle non-finite values.
Results may differ from a plain program's by a relative error of at most 0.025.
Values may be sent and summed in bfloat16 or wider, within the bound.
A program may use at most 128 MiB of HBM per device.

v0:
```python
import jax
import jax.numpy as jnp
from jax import lax
from jax.sharding import PartitionSpec as P

CHANNELS_ONE_HEAD = 64


highest = lax.Precision.HIGHEST


def from_behind(block, axis, distance):
    devices = range(lax.axis_size(axis))
    route = [(i - distance, i) for i in devices if i - distance in devices]
    return lax.ppermute(block, axis, route)


def layer_norm(rows, gain, bias, eps):
    mean = jnp.mean(rows, axis=-1, keepdims=True)
    centred = rows - mean
    spread = jnp.mean(centred * centred, axis=-1, keepdims=True)
    return centred * lax.rsqrt(spread + eps) * gain + bias


def body(
    tier_source_concatenated,
    prompt_sizes_ordered,
    tier_standardize_scale,
    tier_standardize_offset,
    previous_item_mixers,
    mapping_matrices_pile,
    fading_narrow_left,
    fading_narrow_right,
    feature_fading_baseline,
    diagonal_boost_coefficient,
    cluster_standardize_scale,
    cluster_standardize_offset,
    emitted_mapping_matrix,
):
    rows = tier_source_concatenated.shape[0]
    local_width = mapping_matrices_pile.shape[2]
    mixing_values_divided = local_width // CHANNELS_ONE_HEAD
    block = min(32, rows)
    blocks = rows // block
    full = lax.all_gather(tier_source_concatenated, "tp", axis=1, tiled=True)
    normed = layer_norm(
        full.astype(jnp.float32), tier_standardize_scale, tier_standardize_offset, 1e-05
    ).astype(jnp.bfloat16)
    first = jnp.cumsum(prompt_sizes_ordered) - prompt_sizes_ordered
    position = lax.axis_index("seq") * rows + jnp.arange(rows, dtype=jnp.int32)
    is_start = jnp.any(position[:, None] == first[None, :], axis=1)
    segment = jnp.sum((first[None, :] <= position[:, None]).astype(jnp.int32), axis=1)
    edge = from_behind(normed[rows - 1 :], "seq", 1)
    previous = jnp.concatenate([edge, normed[: rows - 1]], axis=0)
    previous = jnp.where(is_start[:, None], jnp.zeros_like(previous), previous)
    base = normed.astype(jnp.float32)
    delta = previous.astype(jnp.float32) - base
    shifted_blend = (base[None] + delta[None] * previous_item_mixers[:, None, :]).astype(
        jnp.bfloat16
    )
    projected = jnp.einsum(
        "itd,ide->ite", shifted_blend[:4], mapping_matrices_pile, preferred_element_type=jnp.float32
    )
    recept = projected[0].astype(jnp.bfloat16)
    key_rows = projected[1].astype(jnp.bfloat16)
    value_rows = projected[2].astype(jnp.bfloat16)
    gate = jax.nn.silu(projected[3]).astype(jnp.bfloat16)
    lowrank_decay_delta = jnp.tanh(
        jnp.dot(shifted_blend[4], fading_narrow_left, preferred_element_type=jnp.float32)
    ).astype(jnp.bfloat16)
    decay_logarithm = -feature_fading_baseline[None, :] * jnp.exp(
        jnp.dot(lowrank_decay_delta, fading_narrow_right, preferred_element_type=jnp.float32)
    )

    def split_heads(values):
        return (
            values.astype(jnp.float32)
            .reshape(blocks, block, mixing_values_divided, CHANNELS_ONE_HEAD)
            .transpose(0, 2, 1, 3)
        )

    inputs = (
        split_heads(recept),
        split_heads(key_rows),
        split_heads(value_rows),
        split_heads(decay_logarithm),
        segment.reshape(blocks, block),
        is_start.astype(jnp.float32).reshape(blocks, block),
    )
    order = jnp.arange(block)
    lower_incl = (order[None, :] <= order[:, None]).astype(jnp.float32)
    strictly = order[None, :] < order[:, None]
    diagonal_extra_contribution = diagonal_boost_coefficient.reshape(
        mixing_values_divided, CHANNELS_ONE_HEAD
    )

    def block_step(carry, item):
        running_recurrence_array, offset, alive = carry
        gating_rows_tile, query_array_tile, content_slab, lw_b, seg_b, start_b = item
        incl = jnp.einsum("ts,hsc->htc", lower_incl, lw_b, precision=highest)
        excl = incl - lw_b
        pair_ok = strictly & (seg_b[None, :] == seg_b[:, None])
        gap = jnp.minimum(excl[:, :, None, :] - incl[:, None, :, :], 0.0)
        weight = jnp.where(pair_ok[None, :, :, None], jnp.exp(gap), 0.0)
        scores = jnp.einsum(
            "htc,hsc,htsc->hts", gating_rows_tile, query_array_tile, weight, precision=highest
        )
        present_item_reward = jnp.sum(
            gating_rows_tile * diagonal_extra_contribution[:, None, :] * query_array_tile, axis=-1
        )
        seen = jnp.dot(lower_incl, start_b, precision=highest)
        valid = (seen == 0.0).astype(jnp.float32)
        carried = gating_rows_tile * jnp.exp(excl) * valid[None, :, None]
        level_ultimate_outcome = (
            jnp.einsum("hts,hsv->htv", scores, content_slab, precision=highest)
            + present_item_reward[..., None] * content_slab
        )
        level_ultimate_outcome = level_ultimate_outcome + jnp.einsum(
            "htc,hcv->htv", carried, running_recurrence_array, precision=highest
        )
        from_start = carried * alive * jnp.exp(offset)[:, None, :]
        total = incl[:, block - 1, :]
        keep = (seen[block - 1] == 0.0).astype(jnp.float32)
        tail_ok = (seg_b == seg_b[block - 1]).astype(jnp.float32)
        tail = query_array_tile * jnp.exp(total[:, None, :] - incl) * tail_ok[None, :, None]
        running_recurrence_array = keep * jnp.exp(total)[
            :, :, None
        ] * running_recurrence_array + jnp.einsum(
            "hsc,hsv->hcv", tail, content_slab, precision=highest
        )
        return (
            (running_recurrence_array, offset + total, alive * keep),
            (level_ultimate_outcome, from_start),
        )

    init = (
        jnp.zeros((mixing_values_divided, CHANNELS_ONE_HEAD, CHANNELS_ONE_HEAD), jnp.float32),
        jnp.zeros((mixing_values_divided, CHANNELS_ONE_HEAD), jnp.float32),
        jnp.float32(1.0),
    )
    (end_state, offset, alive), (outs, from_start) = lax.scan(block_step, init, inputs)
    decay_total = alive * jnp.exp(offset)

    def relay_turn(turn, entering):
        leaving = decay_total[..., None] * entering + end_state
        return from_behind(leaving, "seq", 1)

    incoming = lax.fori_loop(0, lax.axis_size("seq") - 1, relay_turn, jnp.zeros_like(end_state))
    outs = outs + jnp.einsum("bhtc,hcv->bhtv", from_start, incoming, precision=highest)
    wkv = outs.transpose(0, 2, 1, 3).reshape(rows, mixing_values_divided, CHANNELS_ONE_HEAD)
    mean = jnp.mean(wkv, axis=-1, keepdims=True)
    centred = wkv - mean
    spread = jnp.mean(centred * centred, axis=-1, keepdims=True)
    grouped = (centred * lax.rsqrt(spread + 0.00064)).reshape(
        rows, local_width
    ) * cluster_standardize_scale + cluster_standardize_offset
    gated = (grouped * gate.astype(jnp.float32)).astype(jnp.bfloat16)
    partial_sum = jnp.dot(gated, emitted_mapping_matrix, preferred_element_type=jnp.float32)
    summed = lax.psum(partial_sum.astype(jnp.bfloat16), "tp").astype(jnp.float32)
    mine = lax.dynamic_slice_in_dim(summed, lax.axis_index("tp") * local_width, local_width, 1)
    return (tier_source_concatenated.astype(jnp.float32) + mine).astype(jnp.bfloat16)


def solution(mesh):
    in_specs = (
        P("seq", "tp"),
        P(),
        P(),
        P(),
        P(),
        P(None, None, "tp"),
        P(),
        P(None, "tp"),
        P("tp"),
        P("tp"),
        P("tp"),
        P("tp"),
        P("tp", None),
    )
    out_specs = P("seq", "tp")
    return jax.shard_map(body, mesh=mesh, in_specs=in_specs, out_specs=out_specs, check_vma=False)
```

profile of v0, /device:TPU:0, one launch (start us, length us, event | category | flops | bytes accessed | tf_op | source)
XLA Modules:
  0.0 224.9 jit_solution(352860172076934207)
XLA Ops:
  6.5 8.9 %all_gather.3 = bf16[128,2048]{1,0:T(8,128)(2,1)S(1)} all-gather(bf16[128,512]{1,0:T(8,128)(2,1)} %param.17), channel_id=1, replica_groups=mesh['seq'=8,'tp'=4] {'tp'}, dimensions={1}, use_global_device_ids=true | all-gather | bytes 655360 | tf_op jit(solution)/shard_map/all_gather | solution.py:45
  18.1 3.4 %collective-permute-start.1 = (bf16[1,2048]{1,0:T(2,128)(2,1)S(1)}, bf16[1,2048]{1,0:T(2,128)(2,1)S(1)}, u32[]{:S(2)}, u32[]{:S(2)}) collective-permute-start(bf16[1,2048]{1,0:T(2,128)(2,1)S(1)} %slice.52), channel_id=1, source_target_pairs={{0,4},{4,8},{8,12},{12,16},{16,20},{20,24},{24,28},{1,5},{5,9},{9,... | collective-permute-start | bytes 12296 | tf_op jit(solution)/shard_map/ppermute | solution.py:15
  27.8 5.7 %fusion.60 = (bf16[4,128,512]{2,1,0:T(8,128)(2,1)S(1)}, f32[4,128,512]{2,1,0:T(8,128)}) fusion(bf16[4,2048,512]{2,1,0:T(8,128)(2,1)} %param.22, f32[5,2048]{1,0:T(8,128)S(1)} %copy-done.4, f32[128,2048]{1,0:T(8,128)S(1)} %convert_subtract_fusion.1, f32[128,2048]{1,0:T(8,128)S(1)} %copy-done.1), kind=kOutput, calls=%fused_computation.108 | convolution fusion | flops 1077936128 | bytes 12099584 | tf_op jit(solution)/shard_map/itd,ide->ite/dot_general | solution.py:61
  44.3 64.4 %while.31 = (s32[]{:T(128)}, f32[8,64,64]{2,1,0:T(8,128)S(1)}, f32[8,64]{1,0:T(8,128)S(1)}, f32[]{:T(128)}, f32[4,8,32,64]{3,2,0,1:T(8,128)}, /*index=5*/f32[4,8...) while((s32[]{:T(128)}, f32[8,64,64]{2,1,0:T(8,128)S(1)}, ...), condition=%wide.region_7.8_spmd.clone.clone, body=%wide.region_5.7_spmd.clone.clone.sunk | while | flops 41284548 | bytes 7640688 | solution.py:141
  50.4 3.4 %fusion.93 = f32[8,32,32]{1,2,0:T(8,128)S(1)} fusion(f32[8,32,32,64]{3,2,1,0:T(8,128)S(1)} %exponential_select_fusion.2, f32[8,64,32]{1,2,0:T(8,128)S(1)} %get-tuple-element.372, f32[8,64,32]{1,2,0:T(8,128)S(1)} %get-tuple-element.373), kind=kLoop, calls=%fused_computation.5.clone.1 | loop fusion | flops 1564672 | bytes 2260992 | tf_op jit(solution)/shard_map/while/body/eval_jaxpr/htc,hsc,htsc->hts/dot_general | solution.py:105
  66.5 3.4 %fusion.93 = f32[8,32,32]{1,2,0:T(8,128)S(1)} fusion(f32[8,32,32,64]{3,2,1,0:T(8,128)S(1)} %exponential_select_fusion.2, f32[8,64,32]{1,2,0:T(8,128)S(1)} %get-tuple-element.372, f32[8,64,32]{1,2,0:T(8,128)S(1)} %get-tuple-element.373), kind=kLoop, calls=%fused_computation.5.clone.1 | loop fusion | flops 1564672 | bytes 2260992 | tf_op jit(solution)/shard_map/while/body/eval_jaxpr/htc,hsc,htsc->hts/dot_general | solution.py:105
  82.6 3.4 %fusion.93 = f32[8,32,32]{1,2,0:T(8,128)S(1)} fusion(f32[8,32,32,64]{3,2,1,0:T(8,128)S(1)} %exponential_select_fusion.2, f32[8,64,32]{1,2,0:T(8,128)S(1)} %get-tuple-element.372, f32[8,64,32]{1,2,0:T(8,128)S(1)} %get-tuple-element.373), kind=kLoop, calls=%fused_computation.5.clone.1 | loop fusion | flops 1564672 | bytes 2260992 | tf_op jit(solution)/shard_map/while/body/eval_jaxpr/htc,hsc,htsc->hts/dot_general | solution.py:105
  98.7 3.4 %fusion.93 = f32[8,32,32]{1,2,0:T(8,128)S(1)} fusion(f32[8,32,32,64]{3,2,1,0:T(8,128)S(1)} %exponential_select_fusion.2, f32[8,64,32]{1,2,0:T(8,128)S(1)} %get-tuple-element.372, f32[8,64,32]{1,2,0:T(8,128)S(1)} %get-tuple-element.373), kind=kLoop, calls=%fused_computation.5.clone.1 | loop fusion | flops 1564672 | bytes 2260992 | tf_op jit(solution)/shard_map/while/body/eval_jaxpr/htc,hsc,htsc->hts/dot_general | solution.py:105
  108.8 65.2 %while.30 = (s32[]{:T(128)}, f32[8,64,64]{2,1,0:T(8,128)S(1)}, f32[8,64]{1,0:T(8,128)S(1)}, f32[8,64,64]{2,1,0:T(8,128)S(1)}, s32[]{:T(128)}) while((s32[]{:T(128)}, f32[8,64,64]{2,1,0:T(8,128)S(1)}, f32[8,64]{1,0:T(8,128)S(1)}, f32[8,64,64]{2,1,0:T(8,128)S(1)}, s32[]{:T(128)}) %tuple.61), condition=%wide.region_9.10_spmd, body=%wide.region_8.9_spmd.sunk | while | flops 65538 | bytes 919653 | solution.py:148
  108.9 3.6 %collective-permute-start = (f32[8,64,64]{2,1,0:T(8,128)S(1)}, f32[8,64,64]{2,1,0:T(8,128)S(1)}, u32[]{:S(2)}, u32[]{:S(2)}) collective-permute-start(f32[8,64,64]{2,1,0:T(8,128)S(1)} %multiply_add_fusion.2), channel_id=1, source_target_pairs={{0,4},{4,8},{8,12},{12,16},{16,20},{20,24},{24,28},{1,5},{5,9},{9,... | collective-permute-start | bytes 393224 | tf_op jit(solution)/shard_map/while/body/eval_jaxpr/ppermute | solution.py:15
  112.5 5.8 %collective-permute-done = f32[8,64,64]{2,1,0:T(8,128)S(1)} collective-permute-done((f32[8,64,64]{2,1,0:T(8,128)S(1)}, f32[8,64,64]{2,1,0:T(8,128)S(1)}, u32[]{:S(2)}, u32[]{:S(2)}) %collective-permute-start) | collective-permute-done | bytes 131104 | tf_op jit(solution)/shard_map/while/body/eval_jaxpr/ppermute | solution.py:15
  118.4 4.4 %collective-permute-start = (f32[8,64,64]{2,1,0:T(8,128)S(1)}, f32[8,64,64]{2,1,0:T(8,128)S(1)}, u32[]{:S(2)}, u32[]{:S(2)}) collective-permute-start(f32[8,64,64]{2,1,0:T(8,128)S(1)} %multiply_add_fusion.2), channel_id=1, source_target_pairs={{0,4},{4,8},{8,12},{12,16},{16,20},{20,24},{24,28},{1,5},{5,9},{9,... | collective-permute-start | bytes 393224 | tf_op jit(solution)/shard_map/while/body/eval_jaxpr/ppermute | solution.py:15
  122.8 4.9 %collective-permute-done = f32[8,64,64]{2,1,0:T(8,128)S(1)} collective-permute-done((f32[8,64,64]{2,1,0:T(8,128)S(1)}, f32[8,64,64]{2,1,0:T(8,128)S(1)}, u32[]{:S(2)}, u32[]{:S(2)}) %collective-permute-start) | collective-permute-done | bytes 131104 | tf_op jit(solution)/shard_map/while/body/eval_jaxpr/ppermute | solution.py:15
  127.9 4.4 %collective-permute-start = (f32[8,64,64]{2,1,0:T(8,128)S(1)}, f32[8,64,64]{2,1,0:T(8,128)S(1)}, u32[]{:S(2)}, u32[]{:S(2)}) collective-permute-start(f32[8,64,64]{2,1,0:T(8,128)S(1)} %multiply_add_fusion.2), channel_id=1, source_target_pairs={{0,4},{4,8},{8,12},{12,16},{16,20},{20,24},{24,28},{1,5},{5,9},{9,... | collective-permute-start | bytes 393224 | tf_op jit(solution)/shard_map/while/body/eval_jaxpr/ppermute | solution.py:15
  132.3 4.0 %collective-permute-done = f32[8,64,64]{2,1,0:T(8,128)S(1)} collective-permute-done((f32[8,64,64]{2,1,0:T(8,128)S(1)}, f32[8,64,64]{2,1,0:T(8,128)S(1)}, u32[]{:S(2)}, u32[]{:S(2)}) %collective-permute-start) | collective-permute-done | bytes 131104 | tf_op jit(solution)/shard_map/while/body/eval_jaxpr/ppermute | solution.py:15
  136.4 4.6 %collective-permute-start = (f32[8,64,64]{2,1,0:T(8,128)S(1)}, f32[8,64,64]{2,1,0:T(8,128)S(1)}, u32[]{:S(2)}, u32[]{:S(2)}) collective-permute-start(f32[8,64,64]{2,1,0:T(8,128)S(1)} %multiply_add_fusion.2), channel_id=1, source_target_pairs={{0,4},{4,8},{8,12},{12,16},{16,20},{20,24},{24,28},{1,5},{5,9},{9,... | collective-permute-start | bytes 393224 | tf_op jit(solution)/shard_map/while/body/eval_jaxpr/ppermute | solution.py:15
  141.1 3.9 %collective-permute-done = f32[8,64,64]{2,1,0:T(8,128)S(1)} collective-permute-done((f32[8,64,64]{2,1,0:T(8,128)S(1)}, f32[8,64,64]{2,1,0:T(8,128)S(1)}, u32[]{:S(2)}, u32[]{:S(2)}) %collective-permute-start) | collective-permute-done | bytes 131104 | tf_op jit(solution)/shard_map/while/body/eval_jaxpr/ppermute | solution.py:15
  145.0 5.3 %collective-permute-start = (f32[8,64,64]{2,1,0:T(8,128)S(1)}, f32[8,64,64]{2,1,0:T(8,128)S(1)}, u32[]{:S(2)}, u32[]{:S(2)}) collective-permute-start(f32[8,64,64]{2,1,0:T(8,128)S(1)} %multiply_add_fusion.2), channel_id=1, source_target_pairs={{0,4},{4,8},{8,12},{12,16},{16,20},{20,24},{24,28},{1,5},{5,9},{9,... | collective-permute-start | bytes 393224 | tf_op jit(solution)/shard_map/while/body/eval_jaxpr/ppermute | solution.py:15
  150.4 3.9 %collective-permute-done = f32[8,64,64]{2,1,0:T(8,128)S(1)} collective-permute-done((f32[8,64,64]{2,1,0:T(8,128)S(1)}, f32[8,64,64]{2,1,0:T(8,128)S(1)}, u32[]{:S(2)}, u32[]{:S(2)}) %collective-permute-start) | collective-permute-done | bytes 131104 | tf_op jit(solution)/shard_map/while/body/eval_jaxpr/ppermute | solution.py:15
  154.4 5.3 %collective-permute-start = (f32[8,64,64]{2,1,0:T(8,128)S(1)}, f32[8,64,64]{2,1,0:T(8,128)S(1)}, u32[]{:S(2)}, u32[]{:S(2)}) collective-permute-start(f32[8,64,64]{2,1,0:T(8,128)S(1)} %multiply_add_fusion.2), channel_id=1, source_target_pairs={{0,4},{4,8},{8,12},{12,16},{16,20},{20,24},{24,28},{1,5},{5,9},{9,... | collective-permute-start | bytes 393224 | tf_op jit(solution)/shard_map/while/body/eval_jaxpr/ppermute | solution.py:15
  159.7 4.6 %collective-permute-done = f32[8,64,64]{2,1,0:T(8,128)S(1)} collective-permute-done((f32[8,64,64]{2,1,0:T(8,128)S(1)}, f32[8,64,64]{2,1,0:T(8,128)S(1)}, u32[]{:S(2)}, u32[]{:S(2)}) %collective-permute-start) | collective-permute-done | bytes 131104 | tf_op jit(solution)/shard_map/while/body/eval_jaxpr/ppermute | solution.py:15
  164.4 5.7 %collective-permute-start = (f32[8,64,64]{2,1,0:T(8,128)S(1)}, f32[8,64,64]{2,1,0:T(8,128)S(1)}, u32[]{:S(2)}, u32[]{:S(2)}) collective-permute-start(f32[8,64,64]{2,1,0:T(8,128)S(1)} %multiply_add_fusion.2), channel_id=1, source_target_pairs={{0,4},{4,8},{8,12},{12,16},{16,20},{20,24},{24,28},{1,5},{5,9},{9,... | collective-permute-start | bytes 393224 | tf_op jit(solution)/shard_map/while/body/eval_jaxpr/ppermute | solution.py:15
  170.1 3.9 %collective-permute-done = f32[8,64,64]{2,1,0:T(8,128)S(1)} collective-permute-done((f32[8,64,64]{2,1,0:T(8,128)S(1)}, f32[8,64,64]{2,1,0:T(8,128)S(1)}, u32[]{:S(2)}, u32[]{:S(2)}) %collective-permute-start) | collective-permute-done | bytes 131104 | tf_op jit(solution)/shard_map/while/body/eval_jaxpr/ppermute | solution.py:15
  179.4 37.0 %all-reduce.2.cloned.1.call-done = bf16[128,2048]{1,0:T(8,128)(2,1)} async-done(((bf16[128,2048]{1,0:T(8,128)(2,1)}), bf16[128,2048]{1,0:T(8,128)(2,1)}) %all-reduce.2.cloned.1.call-update) | async-done | bytes 524304 | tf_op jit(solution)/shard_map/psum | solution.py:159
  (145 shorter events, 75.3 us)
Async XLA Ops:
  6.5 170.6 %copy-start = (bf16[512,2048]{1,0:T(8,128)(2,1)S(1)}, bf16[512,2048]{1,0:T(8,128)(2,1)}, u32[]{:S(2)}) copy-start(bf16[512,2048]{1,0:T(8,128)(2,1)} %param.29) | copy-start | bytes 6291460
  6.5 17.8 %copy-start.4 = (f32[5,2048]{1,0:T(8,128)S(1)}, f32[5,2048]{1,0:T(8,128)}, u32[]{:S(2)}) copy-start(f32[5,2048]{1,0:T(8,128)} %param.21) | copy-start | bytes 122884
  6.5 209.9 %all-reduce.2.cloned.1.call-start = ((), (), s32[]{:S(2)}) async-start(), calls=%async_computation | async-start | bytes 1048576 | tf_op jit(solution)/shard_map/psum | solution.py:159
  18.1 6.0 %collective-permute-start.1 = (bf16[1,2048]{1,0:T(2,128)(2,1)S(1)}, bf16[1,2048]{1,0:T(2,128)(2,1)S(1)}, u32[]{:S(2)}, u32[]{:S(2)}) collective-permute-start(bf16[1,2048]{1,0:T(2,128)(2,1)S(1)} %slice.52), channel_id=1, source_target_pairs={{0,4},{4,8},{8,12},{12,16},{16,20},{20,24},{24,28},{1,5},{5,9},{9,... | collective-permute-start | bytes 12296 | tf_op jit(solution)/shard_map/ppermute | solution.py:15
  24.1 3.7 %copy-start.1 = (f32[128,2048]{1,0:T(8,128)S(1)}, f32[128,2048]{1,0:T(8,128)}, u32[]{:S(2)}) copy-start(f32[128,2048]{1,0:T(8,128)} %get-tuple-element.233) | copy-start | bytes 3145732
  27.8 9.5 %copy-start.5 = (bf16[64,512]{1,0:T(8,128)(2,1)S(1)}, bf16[64,512]{1,0:T(8,128)(2,1)}, u32[]{:S(2)}) copy-start(bf16[64,512]{1,0:T(8,128)(2,1)} %param.24) | copy-start | bytes 196612
  34.3 10.0 %copy-start.6 = (f32[512]{0:T(512)S(1)}, f32[512]{0:T(512)}, u32[]{:S(2)}) copy-start(f32[512]{0:T(512)} %param.26) | copy-start | bytes 6148
  108.7 65.3 %copy-start.2 = (f32[4,8,32,64]{3,2,0,1:T(8,128)S(1)}, f32[4,8,32,64]{3,2,0,1:T(8,128)}, u32[]{:S(2)}) copy-start(f32[4,8,32,64]{3,2,0,1:T(8,128)} %get-tuple-element.111) | copy-start | bytes 786436
  108.8 68.4 %copy-start.7 = (f32[512]{0:T(512)S(1)}, f32[512]{0:T(512)}, u32[]{:S(2)}) copy-start(f32[512]{0:T(512)} %param.28) | copy-start | bytes 6148
  108.8 68.4 %copy-start.8 = (f32[512]{0:T(512)S(1)}, f32[512]{0:T(512)}, u32[]{:S(2)}) copy-start(f32[512]{0:T(512)} %param.27) | copy-start | bytes 6148
  108.9 9.3 %collective-permute-start = (f32[8,64,64]{2,1,0:T(8,128)S(1)}, f32[8,64,64]{2,1,0:T(8,128)S(1)}, u32[]{:S(2)}, u32[]{:S(2)}) collective-permute-start(f32[8,64,64]{2,1,0:T(8,128)S(1)} %multiply_add_fusion.2), channel_id=1, source_target_pairs={{0,4},{4,8},{8,12},{12,16},{16,20},{20,24},{24,28},{1,5},{5,9},{9,... | collective-permute-start | bytes 393224 | tf_op jit(solution)/shard_map/while/body/eval_jaxpr/ppermute | solution.py:15
  118.4 9.3 %collective-permute-start = (f32[8,64,64]{2,1,0:T(8,128)S(1)}, f32[8,64,64]{2,1,0:T(8,128)S(1)}, u32[]{:S(2)}, u32[]{:S(2)}) collective-permute-start(f32[8,64,64]{2,1,0:T(8,128)S(1)} %multiply_add_fusion.2), channel_id=1, source_target_pairs={{0,4},{4,8},{8,12},{12,16},{16,20},{20,24},{24,28},{1,5},{5,9},{9,... | collective-permute-start | bytes 393224 | tf_op jit(solution)/shard_map/while/body/eval_jaxpr/ppermute | solution.py:15
  127.9 8.4 %collective-permute-start = (f32[8,64,64]{2,1,0:T(8,128)S(1)}, f32[8,64,64]{2,1,0:T(8,128)S(1)}, u32[]{:S(2)}, u32[]{:S(2)}) collective-permute-start(f32[8,64,64]{2,1,0:T(8,128)S(1)} %multiply_add_fusion.2), channel_id=1, source_target_pairs={{0,4},{4,8},{8,12},{12,16},{16,20},{20,24},{24,28},{1,5},{5,9},{9,... | collective-permute-start | bytes 393224 | tf_op jit(solution)/shard_map/while/body/eval_jaxpr/ppermute | solution.py:15
  136.4 8.5 %collective-permute-start = (f32[8,64,64]{2,1,0:T(8,128)S(1)}, f32[8,64,64]{2,1,0:T(8,128)S(1)}, u32[]{:S(2)}, u32[]{:S(2)}) collective-permute-start(f32[8,64,64]{2,1,0:T(8,128)S(1)} %multiply_add_fusion.2), channel_id=1, source_target_pairs={{0,4},{4,8},{8,12},{12,16},{16,20},{20,24},{24,28},{1,5},{5,9},{9,... | collective-permute-start | bytes 393224 | tf_op jit(solution)/shard_map/while/body/eval_jaxpr/ppermute | solution.py:15
  145.0 9.2 %collective-permute-start = (f32[8,64,64]{2,1,0:T(8,128)S(1)}, f32[8,64,64]{2,1,0:T(8,128)S(1)}, u32[]{:S(2)}, u32[]{:S(2)}) collective-permute-start(f32[8,64,64]{2,1,0:T(8,128)S(1)} %multiply_add_fusion.2), channel_id=1, source_target_pairs={{0,4},{4,8},{8,12},{12,16},{16,20},{20,24},{24,28},{1,5},{5,9},{9,... | collective-permute-start | bytes 393224 | tf_op jit(solution)/shard_map/while/body/eval_jaxpr/ppermute | solution.py:15
  154.4 9.9 %collective-permute-start = (f32[8,64,64]{2,1,0:T(8,128)S(1)}, f32[8,64,64]{2,1,0:T(8,128)S(1)}, u32[]{:S(2)}, u32[]{:S(2)}) collective-permute-start(f32[8,64,64]{2,1,0:T(8,128)S(1)} %multiply_add_fusion.2), channel_id=1, source_target_pairs={{0,4},{4,8},{8,12},{12,16},{16,20},{20,24},{24,28},{1,5},{5,9},{9,... | collective-permute-start | bytes 393224 | tf_op jit(solution)/shard_map/while/body/eval_jaxpr/ppermute | solution.py:15
  164.4 9.5 %collective-permute-start = (f32[8,64,64]{2,1,0:T(8,128)S(1)}, f32[8,64,64]{2,1,0:T(8,128)S(1)}, u32[]{:S(2)}, u32[]{:S(2)}) collective-permute-start(f32[8,64,64]{2,1,0:T(8,128)S(1)} %multiply_add_fusion.2), channel_id=1, source_target_pairs={{0,4},{4,8},{8,12},{12,16},{16,20},{20,24},{24,28},{1,5},{5,9},{9,... | collective-permute-start | bytes 393224 | tf_op jit(solution)/shard_map/while/body/eval_jaxpr/ppermute | solution.py:15
  175.7 40.7 %copy-start.3 = (bf16[128,512]{1,0:T(8,128)(2,1)S(1)}, bf16[128,512]{1,0:T(8,128)(2,1)}, u32[]{:S(2)}) copy-start(bf16[128,512]{1,0:T(8,128)(2,1)} %param.17) | copy-start | bytes 393220
Sparse Core Ops, SparseCore 0:
  179.6 36.8 all-reduce.1
where the time goes:
time: 226 us; the launch traced here: 225 us
  waiting for transfers between devices  67.9 us (30%)
  other arithmetic  43.1 us (19%)
  starting transfers between devices  36.7 us (16%)
  matrix products  32.7 us (14%)
  local copies, waits for them, and re-layouts  18.9 us (8%)
  between operations  13.6 us (6%)
  blocking collectives  8.95 us (4%)
  loops' own time  3.08 us (1%)
    psum x1, waiting for transfers between devices, body(): lax.psum(partial_sum.astype(jnp.bfloat16), 'tp').astype(jnp.float32)  37 us
    ppermute x8, starting transfers between devices, from_behind(): return lax.ppermute(block, axis, route)  36.7 us
    ppermute x8, waiting for transfers between devices, from_behind(): return lax.ppermute(block, axis, route)  30.9 us
    dot_general x4, other arithmetic, block_step(): jnp.einsum('htc,hsc,htsc->hts', gating_rows_tile, query_array_tile, weigh...  13.8 us
    all_gather x1, blocking collectives, body(): full = lax.all_gather(tier_source_concatenated, 'tp', axis=1, tiled=True)  8.95 us
    transpose x5, local copies, waits for them, and re-layouts, split_heads(): return values.astype(jnp.float32).reshape(blocks, block, mixing_values_di...  7.38 us
    dynamic_update_slice x4, other arithmetic, body(): lax.scan(block_step, init, inputs)  6.64 us
    dot_general x4, matrix products, block_step(): jnp.einsum('hsc,hsv->hcv', tail, content_slab, precision=highest)  6.64 us
  transfers between devices with their start and end apart: 9, of which 8 were waited for; matrix products, arithmetic and copies ran while one was open for 1% of the time, Pallas kernels for 0%

commit v1 on v0

v1 whole, which is shorter than its diff:
```python
import functools

import jax
import jax.numpy as jnp
import numpy as np
from jax import lax
from jax.experimental import pallas as pl
from jax.experimental.pallas import tpu as pltpu
from jax.sharding import PartitionSpec as P

HEAD = 64
GROUP = 256
EDGE = 16
BF16, F32 = jnp.bfloat16, jnp.float32
NT = (((1,), (1,)), ((), ()))
TN = (((0,), (0,)), ((), ()))


def span_matrix(rows):
    t, j = np.arange(rows)[:, None], np.arange(rows)[None, :]
    parts = []
    for level in range(rows.bit_length() - 1):
        same = (t >> level) == (j >> level)
        odd = ((t >> level) & 1) == 1
        parts.append(same & np.where(odd, j < t, j > t))
    parts += [j < t, j > t, np.ones((16, rows), bool)]
    spans = np.concatenate(parts, 0)
    return np.concatenate([spans, spans], 1).astype(jnp.bfloat16)


def dot(a, b, dims=None):
    if dims is None:
        return jnp.dot(a, b, preferred_element_type=F32)
    return lax.dot_general(a, b, dims, preferred_element_type=F32)


def kernel(
    n, sizes, x, gain, bias, mixers, fading, boost, head_gain, head_bias,
    spans_h, left_h, right_h, pile_h, emitted_h, out,
    xall, edge, spans, left, right, pile, emitted, mixed, rkvg, gated,
    mine, near, far, wide, came, give_far, got_far, give_near, got_near, give_sum, got_sum,
    load_sem, send_sem, recv_sem,
):
    rows, width = x.shape
    levels = rows.bit_length() - 1
    features = 4 * width
    groups = width // GROUP
    per_group = GROUP // HEAD
    s, t = lax.axis_index("seq"), lax.axis_index("tp")
    mate = t + 1 - 2 * lax.rem(t, 2)
    across = t + 2 - 4 * lax.div(t, 2)
    corner = 3 - t

    def ahead(d):
        return lax.rem(s + d, n)

    def behind(d):
        return lax.rem(s + n - d, n)

    loads = [
        (left_h, left), (spans_h, spans), (right_h, right),
        (pile_h.at[1], pile.at[1]), (pile_h.at[2], pile.at[2]),
        (pile_h.at[0], pile.at[0]), (pile_h.at[3], pile.at[3]), (emitted_h, emitted),
    ]
    loads = [pltpu.make_async_copy(a, b, load_sem.at[i]) for i, (a, b) in enumerate(loads)]
    left_in, spans_in, right_in, key_in, value_in, recept_in, gate_in, emitted_in = loads
    for load in loads:
        load.start()

    hops = [1, 2]
    while hops[-1] * 2 < n // 2:
        hops.append(hops[-1] * 2)
    doublings = [d for d in hops if 2 <= d < n // 2]

    barrier = pltpu.get_barrier_semaphore()
    sources = [(s, mate), (s, across)] + [(behind(1), jnp.int32(j)) for j in range(4)]
    sources += [(behind(d), t) for d in hops[1:]]
    for source in sources:
        pl.semaphore_signal(barrier, inc=1, device_id=source, device_id_type=pl.DeviceIdType.MESH)
    pl.semaphore_wait(barrier, len(sources))

    def remote(src, dst, index, device):
        return pltpu.make_async_remote_copy(
            src_ref=src, dst_ref=dst, send_sem=send_sem.at[index], recv_sem=recv_sem.at[index],
            device_id=device, device_id_type=pl.DeviceIdType.MESH,
        )

    over = remote(x, xall.at[t], 0, (s, across))
    over.start()
    side = remote(x, xall.at[t], 1, (s, mate))
    side.start()
    tail_rows = x.at[pl.ds(rows - EDGE, EDGE)]
    edges = [
        remote(tail_rows, edge.at[t], 2 + j, (ahead(1), lax.rem(t + j, 4))) for j in range(4)
    ]
    for copy in edges:
        copy.start()
    xall[t] = x[...]

    firsts = [jnp.int32(0)]
    for i in range(sizes.shape[0] - 1):
        firsts.append(firsts[-1] + sizes[i])

    def prompt_of(position):
        count = jnp.where(firsts[0] <= position, 1, 0)
        for first in firsts[1:]:
            count = count + jnp.where(first <= position, 1, 0)
        return count

    begin = s * rows
    order = lax.broadcasted_iota(jnp.int32, (rows, 1), 0)
    starts = begin + order == firsts[0]
    for first in firsts[1:]:
        starts = starts | (begin + order == first)
    going = jnp.where(starts, 0.0, 1.0)
    prompt = prompt_of(begin + order)
    entering, last = prompt_of(begin - 1), prompt_of(begin + rows - 1)
    valid = jnp.where(prompt == entering, 1.0, 0.0)
    tail_ok = jnp.where(prompt == last, 1.0, 0.0)
    keep = jnp.where(last == entering, 1.0, 0.0)

    over.wait_recv()
    pass_on = remote(xall.at[across], xall.at[across], 6, (s, mate))
    pass_on.start()
    side.wait_recv()
    for copy in edges:
        copy.wait_recv()
    pass_on.wait_recv()

    def moments(ref):
        total = sum(jnp.sum(ref[c].astype(F32), axis=1, keepdims=True) for c in range(4))
        mean = total / features
        square = 0.0
        for c in range(4):
            centred = ref[c].astype(F32) - mean
            square = square + jnp.sum(centred * centred, axis=1, keepdims=True)
        return mean, lax.rsqrt(square / features + 1e-5)

    mean, scale = moments(xall)
    edge_mean, edge_scale = moments(edge)
    for c in range(4):
        cols = slice(c * width, (c + 1) * width)
        base = ((xall[c].astype(F32) - mean) * scale * gain[:, cols] + bias[:, cols])
        base = base.astype(BF16).astype(F32)
        end = ((edge[c].astype(F32) - edge_mean) * edge_scale * gain[:, cols] + bias[:, cols])
        end = end.astype(BF16).astype(F32)
        previous = jnp.where(order == 0, end[EDGE - 1 :, :], pltpu.roll(base, 1, 0)) * going
        delta = previous - base
        for i in range(5):
            mixed[i, :, cols] = (base + delta * mixers[i : i + 1, cols]).astype(BF16)

    left_in.wait()
    right_in.wait()
    lora = jnp.tanh(dot(mixed[4], left[...])).astype(BF16)
    log_decay = -fading[...] * jnp.exp(dot(lora, right[...]))
    high = log_decay.astype(BF16)
    low = (log_decay - high.astype(F32)).astype(BF16)
    pair = jnp.concatenate([high, low], axis=0)
    spans_in.wait()

    def decays(block, lanes, count=rows):
        return jnp.exp(dot(spans[pl.ds(block * rows, count)], pair[:, lanes]))

    key_in.wait()
    rkvg[1] = dot(mixed[1], pile[1]).astype(BF16)
    value_in.wait()
    rkvg[2] = dot(mixed[2], pile[2]).astype(BF16)

    lane = lax.broadcasted_iota(jnp.int32, (1, GROUP), 1)
    of_head = [lane // HEAD == h for h in range(per_group)]
    ones_of = [jnp.where(m, 1.0, 0.0).astype(BF16) for m in of_head]
    all_lanes = [slice(g * GROUP, (g + 1) * GROUP) for g in range(groups)]
    for lanes in all_lanes:
        tail = (rkvg[1, :, lanes].astype(F32) * decays(levels + 1, lanes) * tail_ok).astype(BF16)
        full = dot(rkvg[2, :, lanes], tail, TN)
        state = jnp.where(of_head[0], full[:HEAD], 0.0)
        for h in range(1, per_group):
            state = state + jnp.where(of_head[h], full[h * HEAD : (h + 1) * HEAD], 0.0)
        mine[:HEAD, lanes] = state.astype(BF16)
        mine[HEAD:, lanes] = (decays(levels + 2, lanes, 16) * keep).astype(BF16)
    to_near = remote(mine, near, 7, (ahead(1), t))
    to_near.start()
    to_far = remote(mine, far, 8, (ahead(2), t))
    to_far.start()

    recept_in.wait()
    rkvg[0] = dot(mixed[0], pile[0]).astype(BF16)

    row = lax.broadcasted_iota(jnp.int32, (rows, rows), 0)
    col = lax.broadcasted_iota(jnp.int32, (rows, rows), 1)
    together = prompt_of(begin + row) == prompt_of(begin + col)

    def pair_mask(level):
        if level == levels:
            return jnp.where(row == col, 1.0, 0.0)
        ok = (row >> (level + 1)) == (col >> (level + 1))
        ok = ok & (((row >> level) & 1) == 1) & (((col >> level) & 1) == 0)
        return jnp.where(ok & together, 1.0, 0.0)

    def local_part(lanes):
        recept, key, value = rkvg[0, :, lanes], rkvg[1, :, lanes], rkvg[2, :, lanes]
        scores = [0.0] * per_group
        for level in range(levels + 1):
            if level < levels:
                weight = decays(level, lanes).astype(BF16)
                asks, keys = recept * weight, key * weight
            else:
                asks, keys = (recept.astype(F32) * boost[:, lanes]).astype(BF16), key
            asks = jnp.concatenate([asks * m for m in ones_of], axis=0)
            found = dot(asks, keys, NT)
            mask = pair_mask(level)
            scores = [
                scores[h] + found[h * rows : (h + 1) * rows] * mask for h in range(per_group)
            ]
        scores = jnp.concatenate([p.astype(BF16) for p in scores], axis=1)
        values = jnp.concatenate([value * m for m in ones_of], axis=0)
        return dot(scores, values)

    local = [local_part(all_lanes[0])]

    to_near.wait_recv()
    to_far.wait_recv()
    reach = near[HEAD:].astype(F32)[:1]
    state = near[:HEAD].astype(F32) + reach * far[:HEAD].astype(F32)
    reach = reach * far[HEAD:].astype(F32)[:1]
    sent = []
    for i, d in enumerate(doublings):
        wide[i, :HEAD] = state.astype(BF16)
        wide[i, HEAD:] = jnp.broadcast_to(reach, (16, width)).astype(BF16)
        copy = remote(wide.at[i], came.at[i], 9 + i, (ahead(d), t))
        copy.start()
        sent.append(copy)
        if i == 0:
            local += [local_part(lanes) for lanes in all_lanes[1:]]
            gate_in.wait()
            gate = dot(mixed[3], pile[3])
            rkvg[3] = (gate / (1.0 + jnp.exp(-gate))).astype(BF16)
        copy.wait_recv()
        state = state + reach * came[i, :HEAD].astype(F32)
        reach = reach * came[i, HEAD:].astype(F32)[:1]

    r2 = lax.broadcasted_iota(jnp.int32, (2 * GROUP, GROUP), 0)
    c2 = lax.broadcasted_iota(jnp.int32, (2 * GROUP, GROUP), 1)
    averager = jnp.where(lax.rem(r2, GROUP) // HEAD == c2 // HEAD, 1.0 / HEAD, 0.0).astype(BF16)
    for g, lanes in enumerate(all_lanes):
        carried = (rkvg[0, :, lanes].astype(F32) * decays(levels, lanes) * valid).astype(BF16)
        held = state[:, lanes].astype(BF16)
        held = jnp.concatenate([held * m for m in ones_of], axis=0)
        wkv = local[g] + dot(carried, held, NT)
        big = wkv.astype(BF16)
        small = (wkv - big.astype(F32)).astype(BF16)
        centred = wkv - dot(jnp.concatenate([big, small], axis=1), averager)
        spread = dot((centred * centred).astype(BF16), averager[:GROUP])
        grouped = centred * lax.rsqrt(spread + 6.4e-4) * head_gain[:, lanes] + head_bias[:, lanes]
        gated[:, lanes] = (grouped * rkvg[3, :, lanes].astype(F32)).astype(BF16)

    emitted_in.wait()

    def partial(block):
        return dot(gated[...], emitted[:, pl.ds(pl.multiple_of(block * width, width), width)])

    index = 9 + len(doublings)
    give_far[...] = partial(corner).astype(BF16)
    first_give = remote(give_far, got_far, index, (s, mate))
    first_give.start()
    for_across = partial(across)
    first_give.wait_recv()
    give_sum[...] = (for_across + got_far[...].astype(F32)).astype(BF16)
    sum_give = remote(give_sum, got_sum, index + 1, (s, across))
    sum_give.start()
    give_near[...] = partial(mate).astype(BF16)
    second_give = remote(give_near, got_near, index + 2, (s, mate))
    second_give.start()
    total = x[...].astype(F32) + partial(t)
    second_give.wait_recv()
    total = total + got_near[...].astype(F32)
    sum_give.wait_recv()
    out[...] = (total + got_sum[...].astype(F32)).astype(BF16)

    for copy in [over, side, *edges, pass_on, to_near, to_far, *sent]:
        copy.wait_send()
    for copy in [first_give, sum_give, second_give]:
        copy.wait_send()


def body(n, x, sizes, gain, bias, mixers, pile, left, right, fading, boost, head_gain, head_bias, emitted):
    rows, width = x.shape
    features, rank = left.shape
    doublings = max(1, (n // 2).bit_length() - 2)
    copies = 9 + doublings + 3
    spans = span_matrix(rows)
    vmem, anywhere = pl.BlockSpec(memory_space=pltpu.VMEM), pl.BlockSpec(memory_space=pl.ANY)
    message = pltpu.VMEM((HEAD + 16, width), BF16)
    messages = pltpu.VMEM((doublings, HEAD + 16, width), BF16)
    block = pltpu.VMEM((rows, width), BF16)
    return pl.pallas_call(
        functools.partial(kernel, n),
        out_shape=jax.ShapeDtypeStruct((rows, width), BF16),
        in_specs=[pl.BlockSpec(memory_space=pltpu.SMEM)] + [vmem] * 8 + [anywhere] * 5,
        out_specs=vmem,
        scratch_shapes=[
            pltpu.VMEM((4, rows, width), BF16),
            pltpu.VMEM((4, EDGE, width), BF16),
            pltpu.VMEM(spans.shape, BF16),
            pltpu.VMEM((features, rank), BF16),
            pltpu.VMEM((rank, width), BF16),
            pltpu.VMEM(pile.shape, BF16),
            pltpu.VMEM(emitted.shape, BF16),
            pltpu.VMEM((5, rows, features), BF16),
            pltpu.VMEM((4, rows, width), BF16),
            block,
            message, message, message, messages, messages,
            block, block, block, block, block, block,
            pltpu.SemaphoreType.DMA((8,)),
            pltpu.SemaphoreType.DMA((copies,)),
            pltpu.SemaphoreType.DMA((copies,)),
        ],
        compiler_params=pltpu.CompilerParams(
            collective_id=0, has_side_effects=True, vmem_limit_bytes=48 * 1024 * 1024
        ),
    )(
        sizes, x, gain[None], bias[None], mixers, fading[None], boost[None],
        head_gain[None], head_bias[None], jnp.asarray(spans), left, right, pile, emitted,
    )


def solution(mesh):
    in_specs = (
        P("seq", "tp"), P(), P(), P(), P(), P(None, None, "tp"), P(), P(None, "tp"),
        P("tp"), P("tp"), P("tp"), P("tp"), P("tp", None),
    )
    return jax.shard_map(
        functools.partial(body, mesh.shape["seq"]),
        mesh=mesh, in_specs=in_specs, out_specs=P("seq", "tp"), check_vma=False,
    )
```

time: 226 us -> 44.4 us (0.20)
  waiting for transfers between devices: 67.9 us -> 0 us
  other arithmetic: 43.1 us -> 0 us
  starting transfers between devices: 36.7 us -> 0 us
  matrix products: 32.7 us -> 0 us
  Pallas kernels: 0 us -> 32 us
  between operations: 13.6 us -> 0.04 us
  blocking collectives: 8.95 us -> 0 us
  local copies, waits for them, and re-layouts: 18.9 us -> 11.9 us
  loops' own time: 3.08 us -> 0 us
    psum x1 -> x0, waiting for transfers between devices: 37 us -> none  [body(): lax.psum(partial_sum.astype(jnp.bfloat16), 'tp').astype(jnp.float32)]
    ppermute x8 -> x0, starting transfers between devices: 36.7 us -> none  [from_behind(): return lax.ppermute(block, axis, route)]
    dot_general x24 -> x0, matrix products: 32.7 us -> none  [the longest x4 6.64 us: block_step(): jnp.einsum('hsc,hsv->hcv', tail, content_slab, precision=highest)]
    pallas_call x0 -> x1, Pallas kernels: none -> 32 us  [body(): pl.pallas_call(functools.partial(kernel, n), out_shape=jax.ShapeDtypeStru...]
    ppermute x8 -> x0, waiting for transfers between devices: 30.9 us -> none  [from_behind(): return lax.ppermute(block, axis, route)]
    dot_general x4 -> x0, other arithmetic: 13.8 us -> none  [block_step(): jnp.einsum('htc,hsc,htsc->hts', gating_rows_tile, query_array_tile, weigh...]
    unnamed x18 -> x26, local copies, waits for them, and re-layouts: 0.04 us -> 11.9 us
    convert_element_type x8 -> x0, other arithmetic: 9.67 us -> none  [the longest x1 3.37 us: body(): (base[None] + delta[None] * previous_item_mixers[:, None, :]).astype(jnp....]
  transfers between devices with their start and end apart: 9 -> 0, of which waited for: 8 -> 0; matrix products, arithmetic and copies ran while one was open for 1% -> 0% of each run, Pallas kernels for 0% -> 0%
where the time goes in v1:
time: 44.4 us; the launch traced here: 43.9 us
  Pallas kernels  32 us (72%)
  local copies, waits for them, and re-layouts  11.9 us (27%)
    pallas_call x1, Pallas kernels, body(): pl.pallas_call(functools.partial(kernel, n), out_shape=jax.ShapeDtypeStru...  32 us
    unnamed x26, local copies, waits for them, and re-layouts  11.9 us

profile of v1, /device:TPU:0, one launch (start us, length us, event | category | flops | bytes accessed | tf_op | source)
XLA Modules:
  0.0 43.9 jit_solution(13041280951232711055)
XLA Ops:
  0.0 1.2 %copy.15.left_h = bf16[2048,64]{1,0:T(8,128)(2,1)S(1)} copy(bf16[2048,64]{0,1:T(8,128)(2,1)} %param.20) | data formatting | bytes 524288 | tf_op args[6]
  1.2 0.0 copy-start
  1.2 1.6 %copy-done = bf16[512,2048]{1,0:T(8,128)(2,1)S(1)} copy-done((bf16[512,2048]{1,0:T(8,128)(2,1)S(1)}, bf16[512,2048]{1,0:T(8,128)(2,1)}, u32[]{:S(2)}) %copy-start) | copy-done | bytes 2097176
  2.8 0.0 copy-start.1
  2.8 1.1 %copy-done.1 = bf16[1168,256]{1,0:T(8,128)(2,1)S(1)} copy-done((bf16[1168,256]{1,0:T(8,128)(2,1)S(1)}, bf16[1168,256]{1,0:T(8,128)(2,1)}, u32[]{:S(2)}) %copy-start.1) | copy-done | bytes 598040
  3.9 0.0 copy-start.2
  3.9 0.9 %copy-done.2 = bf16[128,512]{1,0:T(8,128)(2,1)S(1)} copy-done((bf16[128,512]{1,0:T(8,128)(2,1)S(1)}, bf16[128,512]{1,0:T(8,128)(2,1)}, u32[]{:S(2)}) %copy-start.2) | copy-done | bytes 131096
  4.8 0.0 copy-start.3
  4.8 0.8 %copy-done.3 = f32[5,2048]{1,0:T(8,128)S(1)} copy-done((f32[5,2048]{1,0:T(8,128)S(1)}, f32[5,2048]{1,0:T(8,128)}, u32[]{:S(2)}) %copy-start.3) | copy-done | bytes 40984
  5.6 0.0 copy-start.4
  5.6 0.8 %copy-done.4 = bf16[64,512]{1,0:T(8,128)(2,1)S(1)} copy-done((bf16[64,512]{1,0:T(8,128)(2,1)S(1)}, bf16[64,512]{1,0:T(8,128)(2,1)}, u32[]{:S(2)}) %copy-start.4) | copy-done | bytes 65560
  6.5 0.0 copy-start.5
  6.5 0.7 %copy-done.5 = f32[2048]{0:T(1024)S(1)} copy-done((f32[2048]{0:T(1024)S(1)}, f32[2048]{0:T(1024)}, u32[]{:S(2)}) %copy-start.5) | copy-done | bytes 8216
  7.2 0.0 copy-start.6
  7.2 0.7 %copy-done.6 = f32[2048]{0:T(1024)S(1)} copy-done((f32[2048]{0:T(1024)S(1)}, f32[2048]{0:T(1024)}, u32[]{:S(2)}) %copy-start.6) | copy-done | bytes 8216
  7.9 0.0 copy-start.7
  7.9 0.7 %copy-done.7 = f32[512]{0:T(512)S(1)} copy-done((f32[512]{0:T(512)S(1)}, f32[512]{0:T(512)}, u32[]{:S(2)}) %copy-start.7) | copy-done | bytes 2072
  8.6 0.0 copy-start.8
  8.6 0.7 %copy-done.8 = f32[512]{0:T(512)S(1)} copy-done((f32[512]{0:T(512)S(1)}, f32[512]{0:T(512)}, u32[]{:S(2)}) %copy-start.8) | copy-done | bytes 2072
  9.2 0.7 %copy-done.9 = f32[512]{0:T(512)S(1)} copy-done((f32[512]{0:T(512)S(1)}, f32[512]{0:T(512)}, u32[]{:S(2)}) %copy-start.9) | copy-done | bytes 2072
  9.9 0.7 %copy-done.10 = f32[512]{0:T(512)S(1)} copy-done((f32[512]{0:T(512)S(1)}, f32[512]{0:T(512)}, u32[]{:S(2)}) %copy-start.10) | copy-done | bytes 2072
  10.6 0.7 %copy-done.11 = s32[4]{0:T(128)S(1)} copy-done((s32[4]{0:T(128)S(1)}, s32[4]{0:T(128)}, u32[]{:S(2)}) %copy-start.11) | copy-done | bytes 40
  11.3 32.0 %shard_map.136 = bf16[128,512]{1,0:T(8,128)(2,1)S(1)} custom-call(s32[4]{0:T(128)S(1)} %copy-done.11, bf16[128,512]{1,0:T(8,128)(2,1)S(1)} %copy-done.2, f32[1,2048]{1,0:T(1,128)S(1)} %bitcast.6, f32[1,2048]{1,0:T(1,128)S(1)} %bitcast.7, f32[5,2048]{1,0:T(8,128)S(1)} %copy-done.3, f32[1,512]{1,0:T(1,128)S(1)} %bitcast.8, f32[1,512]{1,0:T(1,128)S(1)} %bitcast.9, ...), custom_call_target="tpu_custom_call" | custom-call | tf_op jit(solution)/shard_map/pallas_call | solution.py:296
  43.3 0.7 %copy.17 = bf16[128,512]{1,0:T(8,128)(2,1)} copy(bf16[128,512]{1,0:T(8,128)(2,1)S(1)} %shard_map.136) | data formatting | bytes 262144
  (3 shorter events, 0.0 us)
Async XLA Ops:
  1.2 1.6 %copy-start = (bf16[512,2048]{1,0:T(8,128)(2,1)S(1)}, bf16[512,2048]{1,0:T(8,128)(2,1)}, u32[]{:S(2)}) copy-start(bf16[512,2048]{1,0:T(8,128)(2,1)} %emitted_h.1) | copy-start | bytes 6291460
  2.8 1.1 %copy-start.1 = (bf16[1168,256]{1,0:T(8,128)(2,1)S(1)}, bf16[1168,256]{1,0:T(8,128)(2,1)}, u32[]{:S(2)}) copy-start(bf16[1168,256]{1,0:T(8,128)(2,1)} %constant.2.clone.spans_h) | copy-start | bytes 1794052
  3.9 0.9 %copy-start.2 = (bf16[128,512]{1,0:T(8,128)(2,1)S(1)}, bf16[128,512]{1,0:T(8,128)(2,1)}, u32[]{:S(2)}) copy-start(bf16[128,512]{1,0:T(8,128)(2,1)} %x.1) | copy-start | bytes 393220
  4.8 0.8 %copy-start.3 = (f32[5,2048]{1,0:T(8,128)S(1)}, f32[5,2048]{1,0:T(8,128)}, u32[]{:S(2)}) copy-start(f32[5,2048]{1,0:T(8,128)} %mixers.1) | copy-start | bytes 122884
  5.6 0.8 %copy-start.4 = (bf16[64,512]{1,0:T(8,128)(2,1)S(1)}, bf16[64,512]{1,0:T(8,128)(2,1)}, u32[]{:S(2)}) copy-start(bf16[64,512]{1,0:T(8,128)(2,1)} %right_h.1) | copy-start | bytes 196612
  6.5 0.7 %copy-start.5 = (f32[2048]{0:T(1024)S(1)}, f32[2048]{0:T(1024)}, u32[]{:S(2)}) copy-start(f32[2048]{0:T(1024)} %param.16) | copy-start | bytes 24580
  7.2 0.7 %copy-start.6 = (f32[2048]{0:T(1024)S(1)}, f32[2048]{0:T(1024)}, u32[]{:S(2)}) copy-start(f32[2048]{0:T(1024)} %param.17) | copy-start | bytes 24580
  7.9 0.7 %copy-start.7 = (f32[512]{0:T(512)S(1)}, f32[512]{0:T(512)}, u32[]{:S(2)}) copy-start(f32[512]{0:T(512)} %param.22) | copy-start | bytes 6148
  8.6 0.7 %copy-start.8 = (f32[512]{0:T(512)S(1)}, f32[512]{0:T(512)}, u32[]{:S(2)}) copy-start(f32[512]{0:T(512)} %param.23) | copy-start | bytes 6148
  9.2 0.7 %copy-start.9 = (f32[512]{0:T(512)S(1)}, f32[512]{0:T(512)}, u32[]{:S(2)}) copy-start(f32[512]{0:T(512)} %param.24) | copy-start | bytes 6148
  9.9 0.7 %copy-start.10 = (f32[512]{0:T(512)S(1)}, f32[512]{0:T(512)}, u32[]{:S(2)}) copy-start(f32[512]{0:T(512)} %param.25) | copy-start | bytes 6148
  10.6 0.7 %copy-start.11 = (s32[4]{0:T(128)S(1)}, s32[4]{0:T(128)}, u32[]{:S(2)}) copy-start(s32[4]{0:T(128)} %sizes.1) | copy-start | bytes 52

commit v2 on v1

--- a/solution.py
+++ b/solution.py
@@ -35,9 +35,9 @@
 
 
 def kernel(
-    n, sizes, x, gain, bias, mixers, fading, boost, head_gain, head_bias,
+    n, sizes_h, x, gain_h, bias_h, mixers_h, fading_h, boost_h, head_gain_h, head_bias_h,
     spans_h, left_h, right_h, pile_h, emitted_h, out,
-    xall, edge, spans, left, right, pile, emitted, mixed, rkvg, gated,
+    sizes, gain, bias, mixers, fading, boost, head_gain, head_bias, xall, edge, spans, left, right, pile, emitted, mixed, rkvg, gated,
     mine, near, far, wide, came, give_far, got_far, give_near, got_near, give_sum, got_sum,
     load_sem, send_sem, recv_sem,
 ):
@@ -57,15 +57,21 @@
     def behind(d):
         return lax.rem(s + n - d, n)
 
-    loads = [
-        (left_h, left), (spans_h, spans), (right_h, right),
-        (pile_h.at[1], pile.at[1]), (pile_h.at[2], pile.at[2]),
-        (pile_h.at[0], pile.at[0]), (pile_h.at[3], pile.at[3]), (emitted_h, emitted),
+    wanted = [
+        (x, xall.at[t]), (sizes_h, sizes), (gain_h, gain), (bias_h, bias), (mixers_h, mixers),
+        (left_h, left), (right_h, right), (fading_h, fading), (spans_h, spans),
+        (pile_h.at[1], pile.at[1]), (pile_h.at[2], pile.at[2]), (pile_h.at[0], pile.at[0]),
+        (boost_h, boost), (pile_h.at[3], pile.at[3]), (head_gain_h, head_gain),
+        (head_bias_h, head_bias), (emitted_h, emitted),
     ]
-    loads = [pltpu.make_async_copy(a, b, load_sem.at[i]) for i, (a, b) in enumerate(loads)]
-    left_in, spans_in, right_in, key_in, value_in, recept_in, gate_in, emitted_in = loads
+    loads = [pltpu.make_async_copy(a, b, load_sem.at[i]) for i, (a, b) in enumerate(wanted)]
     for load in loads:
         load.start()
+    unread = list(loads)
+
+    def ready(upto):
+        while len(loads) - len(unread) < upto:
+            unread.pop(0).wait()
 
     hops = [1, 2]
     while hops[-1] * 2 < n // 2:
@@ -95,7 +101,7 @@
     ]
     for copy in edges:
         copy.start()
-    xall[t] = x[...]
+    ready(2)
 
     firsts = [jnp.int32(0)]
     for i in range(sizes.shape[0] - 1):
@@ -126,6 +132,9 @@
     for copy in edges:
         copy.wait_recv()
     pass_on.wait_recv()
+
+
+    ready(5)
 
     def moments(ref):
         total = sum(jnp.sum(ref[c].astype(F32), axis=1, keepdims=True) for c in range(4))
@@ -149,22 +158,23 @@
         for i in range(5):
             mixed[i, :, cols] = (base + delta * mixers[i : i + 1, cols]).astype(BF16)
 
-    left_in.wait()
-    right_in.wait()
-    lora = jnp.tanh(dot(mixed[4], left[...])).astype(BF16)
+
+    ready(9)
+    lora = jnp.tanh(dot(mixed[4], left[...], NT)).astype(BF16)
     log_decay = -fading[...] * jnp.exp(dot(lora, right[...]))
     high = log_decay.astype(BF16)
     low = (log_decay - high.astype(F32)).astype(BF16)
     pair = jnp.concatenate([high, low], axis=0)
-    spans_in.wait()
 
     def decays(block, lanes, count=rows):
         return jnp.exp(dot(spans[pl.ds(block * rows, count)], pair[:, lanes]))
 
-    key_in.wait()
+
+    ready(10)
     rkvg[1] = dot(mixed[1], pile[1]).astype(BF16)
-    value_in.wait()
+    ready(11)
     rkvg[2] = dot(mixed[2], pile[2]).astype(BF16)
+
 
     lane = lax.broadcasted_iota(jnp.int32, (1, GROUP), 1)
     of_head = [lane // HEAD == h for h in range(per_group)]
@@ -183,8 +193,10 @@
     to_far = remote(mine, far, 8, (ahead(2), t))
     to_far.start()
 
-    recept_in.wait()
+
+    ready(13)
     rkvg[0] = dot(mixed[0], pile[0]).astype(BF16)
+
 
     row = lax.broadcasted_iota(jnp.int32, (rows, rows), 0)
     col = lax.broadcasted_iota(jnp.int32, (rows, rows), 1)
@@ -218,8 +230,10 @@
 
     local = [local_part(all_lanes[0])]
 
+
     to_near.wait_recv()
     to_far.wait_recv()
+
     reach = near[HEAD:].astype(F32)[:1]
     state = near[:HEAD].astype(F32) + reach * far[:HEAD].astype(F32)
     reach = reach * far[HEAD:].astype(F32)[:1]
@@ -232,13 +246,15 @@
         sent.append(copy)
         if i == 0:
             local += [local_part(lanes) for lanes in all_lanes[1:]]
-            gate_in.wait()
+            ready(14)
             gate = dot(mixed[3], pile[3])
             rkvg[3] = (gate / (1.0 + jnp.exp(-gate))).astype(BF16)
         copy.wait_recv()
         state = state + reach * came[i, :HEAD].astype(F32)
         reach = reach * came[i, HEAD:].astype(F32)[:1]
 
+
+    ready(16)
     r2 = lax.broadcasted_iota(jnp.int32, (2 * GROUP, GROUP), 0)
     c2 = lax.broadcasted_iota(jnp.int32, (2 * GROUP, GROUP), 1)
     averager = jnp.where(lax.rem(r2, GROUP) // HEAD == c2 // HEAD, 1.0 / HEAD, 0.0).astype(BF16)
@@ -254,7 +270,8 @@
         grouped = centred * lax.rsqrt(spread + 6.4e-4) * head_gain[:, lanes] + head_bias[:, lanes]
         gated[:, lanes] = (grouped * rkvg[3, :, lanes].astype(F32)).astype(BF16)
 
-    emitted_in.wait()
+
+    ready(17)
 
     def partial(block):
         return dot(gated[...], emitted[:, pl.ds(pl.multiple_of(block * width, width), width)])
@@ -271,7 +288,7 @@
     give_near[...] = partial(mate).astype(BF16)
     second_give = remote(give_near, got_near, index + 2, (s, mate))
     second_give.start()
-    total = x[...].astype(F32) + partial(t)
+    total = xall[t].astype(F32) + partial(t)
     second_give.wait_recv()
     total = total + got_near[...].astype(F32)
     sum_give.wait_recv()
@@ -289,20 +306,23 @@
     doublings = max(1, (n // 2).bit_length() - 2)
     copies = 9 + doublings + 3
     spans = span_matrix(rows)
-    vmem, anywhere = pl.BlockSpec(memory_space=pltpu.VMEM), pl.BlockSpec(memory_space=pl.ANY)
+    vmem, hbm = pl.BlockSpec(memory_space=pltpu.VMEM), pl.BlockSpec(memory_space=pltpu.HBM)
     message = pltpu.VMEM((HEAD + 16, width), BF16)
     messages = pltpu.VMEM((doublings, HEAD + 16, width), BF16)
     block = pltpu.VMEM((rows, width), BF16)
+    whole, part = pltpu.VMEM((1, features), F32), pltpu.VMEM((1, width), F32)
     return pl.pallas_call(
         functools.partial(kernel, n),
         out_shape=jax.ShapeDtypeStruct((rows, width), BF16),
-        in_specs=[pl.BlockSpec(memory_space=pltpu.SMEM)] + [vmem] * 8 + [anywhere] * 5,
+        in_specs=[hbm] * 14,
         out_specs=vmem,
         scratch_shapes=[
+            pltpu.SMEM(sizes.shape, jnp.int32),
+            whole, whole, pltpu.VMEM(mixers.shape, F32), part, part, part, part,
             pltpu.VMEM((4, rows, width), BF16),
             pltpu.VMEM((4, EDGE, width), BF16),
             pltpu.VMEM(spans.shape, BF16),
-            pltpu.VMEM((features, rank), BF16),
+            pltpu.VMEM((rank, features), BF16),
             pltpu.VMEM((rank, width), BF16),
             pltpu.VMEM(pile.shape, BF16),
             pltpu.VMEM(emitted.shape, BF16),
@@ -311,16 +331,16 @@
             block,
             message, message, message, messages, messages,
             block, block, block, block, block, block,
-            pltpu.SemaphoreType.DMA((8,)),
+            pltpu.SemaphoreType.DMA((17,)),
             pltpu.SemaphoreType.DMA((copies,)),
             pltpu.SemaphoreType.DMA((copies,)),
         ],
         compiler_params=pltpu.CompilerParams(
-            collective_id=0, has_side_effects=True, vmem_limit_bytes=48 * 1024 * 1024
+            collective_id=0, has_side_effects=True, vmem_limit_bytes=63 * 1024 * 1024
         ),
     )(
         sizes, x, gain[None], bias[None], mixers, fading[None], boost[None],
-        head_gain[None], head_bias[None], jnp.asarray(spans), left, right, pile, emitted,
+        head_gain[None], head_bias[None], jnp.asarray(spans), left.T, right, pile, emitted,
     )
 
 

time: 44.4 us -> 34 us (0.77)
  local copies, waits for them, and re-layouts: 11.9 us -> 1.57 us
    unnamed x26 -> x1, local copies, waits for them, and re-layouts: 11.9 us -> 1.57 us
where the time goes in v2:
time: 34 us; the launch traced here: 33.8 us
  Pallas kernels  32.3 us (95%)
  local copies, waits for them, and re-layouts  1.57 us (5%)
    pallas_call x1, Pallas kernels, body(): pl.pallas_call(functools.partial(kernel, n), out_shape=jax.ShapeDtypeStru...  32.3 us
    unnamed x1, local copies, waits for them, and re-layouts  1.57 us

profile of v2, /device:TPU:0, one launch (start us, length us, event | category | flops | bytes accessed | tf_op | source)
XLA Modules:
  0.0 33.8 jit_solution(18443267316022429993)
XLA Ops:
  0.0 32.3 %shard_map.136 = bf16[128,512]{1,0:T(8,128)(2,1)} custom-call(s32[4]{0:T(128)} %sizes_h.1, bf16[128,512]{1,0:T(8,128)(2,1)} %x.1, f32[1,2048]{1,0:T(1,128)} %bitcast.8, f32[1,2048]{1,0:T(1,128)} %bitcast.9, f32[5,2048]{1,0:T(8,128)} %mixers_h.1, f32[1,512]{1,0:T(1,128)} %bitcast.10, f32[1,512]{1,0:T(1,128)} %bitcast.11, f32[1,512]{1,0:T(1,128)} %bitcast.12, ...), custom_call_target="tpu_custom_call" | custom-call | tf_op jit(solution)/shard_map/pallas_call | solution.py:314
  32.3 1.6 %copy.16 = bf16[128,512]{1,0:T(8,128)(2,1)} copy(bf16[128,512]{1,0:T(8,128)(2,1)} %shard_map.136) | data formatting | bytes 262144

commit v3 on v2

--- a/solution.py
+++ b/solution.py
@@ -57,21 +57,39 @@
     def behind(d):
         return lax.rem(s + n - d, n)
 
+    def quarters(index):
+        step = pile.shape[1] // 4
+        cut = [pl.ds(i * step, step) for i in range(4)]
+        return [(pile_h.at[index, part], pile.at[index, part]) for part in cut]
+
     wanted = [
-        (x, xall.at[t]), (sizes_h, sizes), (gain_h, gain), (bias_h, bias), (mixers_h, mixers),
-        (left_h, left), (right_h, right), (fading_h, fading), (spans_h, spans),
-        (pile_h.at[1], pile.at[1]), (pile_h.at[2], pile.at[2]), (pile_h.at[0], pile.at[0]),
-        (boost_h, boost), (pile_h.at[3], pile.at[3]), (head_gain_h, head_gain),
-        (head_bias_h, head_bias), (emitted_h, emitted),
+        [(x, xall.at[t])], [(sizes_h, sizes)],
+        [(gain_h, gain)], [(bias_h, bias)], [(mixers_h, mixers)],
+        [(left_h, left)], [(right_h, right)], [(fading_h, fading)], [(spans_h, spans)],
+        quarters(1), quarters(2), quarters(0),
+        [(boost_h, boost)], quarters(3), [(head_gain_h, head_gain)],
+        [(head_bias_h, head_bias)], [(emitted_h, emitted)],
     ]
-    loads = [pltpu.make_async_copy(a, b, load_sem.at[i]) for i, (a, b) in enumerate(wanted)]
-    for load in loads:
-        load.start()
+    loads, used = [], 0
+    for entry in wanted:
+        loads.append([
+            pltpu.make_async_copy(a, b, load_sem.at[used + i]) for i, (a, b) in enumerate(entry)
+        ])
+        used += len(entry)
+
+    def begin_loads(first, end):
+        for entry in loads[first:end]:
+            for load in entry:
+                load.start()
+
     unread = list(loads)
 
     def ready(upto):
         while len(loads) - len(unread) < upto:
-            unread.pop(0).wait()
+            for load in unread.pop(0):
+                load.wait()
+
+    begin_loads(0, 11)
 
     hops = [1, 2]
     while hops[-1] * 2 < n // 2:
@@ -126,6 +144,7 @@
     keep = jnp.where(last == entering, 1.0, 0.0)
 
     over.wait_recv()
+    begin_loads(11, len(loads))
     pass_on = remote(xall.at[across], xall.at[across], 6, (s, mate))
     pass_on.start()
     side.wait_recv()
@@ -331,7 +350,7 @@
             block,
             message, message, message, messages, messages,
             block, block, block, block, block, block,
-            pltpu.SemaphoreType.DMA((17,)),
+            pltpu.SemaphoreType.DMA((29,)),
             pltpu.SemaphoreType.DMA((copies,)),
             pltpu.SemaphoreType.DMA((copies,)),
         ],

time: 34 us -> 34.1 us (level)
  no operation moved by 1% of the time
where the time goes in v3:
time: 34.1 us; the launch traced here: 34 us
  Pallas kernels  32.4 us (95%)
  local copies, waits for them, and re-layouts  1.57 us (5%)
    pallas_call x1, Pallas kernels, body(): pl.pallas_call(functools.partial(kernel, n), out_shape=jax.ShapeDtypeStru...  32.4 us
    unnamed x1, local copies, waits for them, and re-layouts  1.57 us

profile of v3, /device:TPU:0, one launch (start us, length us, event | category | flops | bytes accessed | tf_op | source)
XLA Modules:
  0.0 34.0 jit_solution(2138819153907135820)
XLA Ops:
  0.0 32.4 %shard_map.136 = bf16[128,512]{1,0:T(8,128)(2,1)} custom-call(s32[4]{0:T(128)} %sizes_h.1, bf16[128,512]{1,0:T(8,128)(2,1)} %x.1, f32[1,2048]{1,0:T(1,128)} %bitcast.8, f32[1,2048]{1,0:T(1,128)} %bitcast.9, f32[5,2048]{1,0:T(8,128)} %mixers_h.1, f32[1,512]{1,0:T(1,128)} %bitcast.10, f32[1,512]{1,0:T(1,128)} %bitcast.11, f32[1,512]{1,0:T(1,128)} %bitcast.12, ...), custom_call_target="tpu_custom_call" | custom-call | tf_op jit(solution)/shard_map/pallas_call | solution.py:333
  32.4 1.6 %copy.16 = bf16[128,512]{1,0:T(8,128)(2,1)} copy(bf16[128,512]{1,0:T(8,128)(2,1)} %shard_map.136) | data formatting | bytes 262144

commit v4 on v2

--- a/solution.py
+++ b/solution.py
@@ -180,19 +180,19 @@
     of_head = [lane // HEAD == h for h in range(per_group)]
     ones_of = [jnp.where(m, 1.0, 0.0).astype(BF16) for m in of_head]
     all_lanes = [slice(g * GROUP, (g + 1) * GROUP) for g in range(groups)]
-    for lanes in all_lanes:
+    to_near, to_far = [], []
+    for g, lanes in enumerate(all_lanes):
         tail = (rkvg[1, :, lanes].astype(F32) * decays(levels + 1, lanes) * tail_ok).astype(BF16)
         full = dot(rkvg[2, :, lanes], tail, TN)
         state = jnp.where(of_head[0], full[:HEAD], 0.0)
         for h in range(1, per_group):
             state = state + jnp.where(of_head[h], full[h * HEAD : (h + 1) * HEAD], 0.0)
-        mine[:HEAD, lanes] = state.astype(BF16)
-        mine[HEAD:, lanes] = (decays(levels + 2, lanes, 16) * keep).astype(BF16)
-    to_near = remote(mine, near, 7, (ahead(1), t))
-    to_near.start()
-    to_far = remote(mine, far, 8, (ahead(2), t))
-    to_far.start()
-
+        mine[g, :HEAD] = state.astype(BF16)
+        mine[g, HEAD:] = (decays(levels + 2, lanes, 16) * keep).astype(BF16)
+        to_near.append(remote(mine.at[g], near.at[g], 7 + g, (ahead(1), t)))
+        to_near[g].start()
+        to_far.append(remote(mine.at[g], far.at[g], 7 + groups + g, (ahead(2), t)))
+        to_far[g].start()
 
     ready(13)
     rkvg[0] = dot(mixed[0], pile[0]).astype(BF16)
@@ -231,36 +231,43 @@
     local = [local_part(all_lanes[0])]
 
 
-    to_near.wait_recv()
-    to_far.wait_recv()
-
-    reach = near[HEAD:].astype(F32)[:1]
-    state = near[:HEAD].astype(F32) + reach * far[:HEAD].astype(F32)
-    reach = reach * far[HEAD:].astype(F32)[:1]
-    sent = []
+    base_index = 7 + 2 * groups
+    state, reach, sent = [None] * groups, [None] * groups, []
+
+    def fold(i, g):
+        sent[i * groups + g].wait_recv()
+        state[g] = state[g] + reach[g] * came[i, g, :HEAD].astype(F32)
+        reach[g] = reach[g] * came[i, g, HEAD:].astype(F32)[:1]
+
     for i, d in enumerate(doublings):
-        wide[i, :HEAD] = state.astype(BF16)
-        wide[i, HEAD:] = jnp.broadcast_to(reach, (16, width)).astype(BF16)
-        copy = remote(wide.at[i], came.at[i], 9 + i, (ahead(d), t))
-        copy.start()
-        sent.append(copy)
+        for g in range(groups):
+            if i == 0:
+                to_near[g].wait_recv()
+                to_far[g].wait_recv()
+                by_near = near[g, HEAD:].astype(F32)[:1]
+                state[g] = near[g, :HEAD].astype(F32) + by_near * far[g, :HEAD].astype(F32)
+                reach[g] = by_near * far[g, HEAD:].astype(F32)[:1]
+            else:
+                fold(i - 1, g)
+            wide[i, g, :HEAD] = state[g].astype(BF16)
+            wide[i, g, HEAD:] = jnp.broadcast_to(reach[g], (16, GROUP)).astype(BF16)
+            place = base_index + i * groups + g
+            sent.append(remote(wide.at[i, g], came.at[i, g], place, (ahead(d), t)))
+            sent[-1].start()
         if i == 0:
             local += [local_part(lanes) for lanes in all_lanes[1:]]
             ready(14)
             gate = dot(mixed[3], pile[3])
             rkvg[3] = (gate / (1.0 + jnp.exp(-gate))).astype(BF16)
-        copy.wait_recv()
-        state = state + reach * came[i, :HEAD].astype(F32)
-        reach = reach * came[i, HEAD:].astype(F32)[:1]
-
 
     ready(16)
     r2 = lax.broadcasted_iota(jnp.int32, (2 * GROUP, GROUP), 0)
     c2 = lax.broadcasted_iota(jnp.int32, (2 * GROUP, GROUP), 1)
     averager = jnp.where(lax.rem(r2, GROUP) // HEAD == c2 // HEAD, 1.0 / HEAD, 0.0).astype(BF16)
     for g, lanes in enumerate(all_lanes):
+        fold(len(doublings) - 1, g)
         carried = (rkvg[0, :, lanes].astype(F32) * decays(levels, lanes) * valid).astype(BF16)
-        held = state[:, lanes].astype(BF16)
+        held = state[g].astype(BF16)
         held = jnp.concatenate([held * m for m in ones_of], axis=0)
         wkv = local[g] + dot(carried, held, NT)
         big = wkv.astype(BF16)
@@ -276,7 +283,7 @@
     def partial(block):
         return dot(gated[...], emitted[:, pl.ds(pl.multiple_of(block * width, width), width)])
 
-    index = 9 + len(doublings)
+    index = base_index + groups * len(doublings)
     give_far[...] = partial(corner).astype(BF16)
     first_give = remote(give_far, got_far, index, (s, mate))
     first_give.start()
@@ -294,7 +301,7 @@
     sum_give.wait_recv()
     out[...] = (total + got_sum[...].astype(F32)).astype(BF16)
 
-    for copy in [over, side, *edges, pass_on, to_near, to_far, *sent]:
+    for copy in [over, side, *edges, pass_on, *to_near, *to_far, *sent]:
         copy.wait_send()
     for copy in [first_give, sum_give, second_give]:
         copy.wait_send()
@@ -304,11 +311,12 @@
     rows, width = x.shape
     features, rank = left.shape
     doublings = max(1, (n // 2).bit_length() - 2)
-    copies = 9 + doublings + 3
+    groups = width // GROUP
+    copies = 7 + groups * (2 + doublings) + 3
     spans = span_matrix(rows)
     vmem, hbm = pl.BlockSpec(memory_space=pltpu.VMEM), pl.BlockSpec(memory_space=pltpu.HBM)
-    message = pltpu.VMEM((HEAD + 16, width), BF16)
-    messages = pltpu.VMEM((doublings, HEAD + 16, width), BF16)
+    message = pltpu.VMEM((groups, HEAD + 16, GROUP), BF16)
+    messages = pltpu.VMEM((doublings, groups, HEAD + 16, GROUP), BF16)
     block = pltpu.VMEM((rows, width), BF16)
     whole, part = pltpu.VMEM((1, features), F32), pltpu.VMEM((1, width), F32)
     return pl.pallas_call(

time: 34 us -> 33.2 us (0.976)
  Pallas kernels: 32.3 us -> 31.5 us
    pallas_call x1, Pallas kernels: 32.3 us -> 31.5 us  [body(): pl.pallas_call(functools.partial(kernel, n), out_shape=jax.ShapeDtypeStru...]
where the time goes in v4:
time: 33.2 us; the launch traced here: 33.1 us
  Pallas kernels  31.5 us (95%)
  local copies, waits for them, and re-layouts  1.57 us (5%)
    pallas_call x1, Pallas kernels, body(): pl.pallas_call(functools.partial(kernel, n), out_shape=jax.ShapeDtypeStru...  31.5 us
    unnamed x1, local copies, waits for them, and re-layouts  1.57 us

profile of v4, /device:TPU:0, one launch (start us, length us, event | category | flops | bytes accessed | tf_op | source)
XLA Modules:
  0.0 33.1 jit_solution(12069776000073106943)
XLA Ops:
  0.0 31.5 %shard_map.136 = bf16[128,512]{1,0:T(8,128)(2,1)} custom-call(s32[4]{0:T(128)} %sizes_h.1, bf16[128,512]{1,0:T(8,128)(2,1)} %x.1, f32[1,2048]{1,0:T(1,128)} %bitcast.8, f32[1,2048]{1,0:T(1,128)} %bitcast.9, f32[5,2048]{1,0:T(8,128)} %mixers_h.1, f32[1,512]{1,0:T(1,128)} %bitcast.10, f32[1,512]{1,0:T(1,128)} %bitcast.11, f32[1,512]{1,0:T(1,128)} %bitcast.12, ...), custom_call_target="tpu_custom_call" | custom-call | tf_op jit(solution)/shard_map/pallas_call | solution.py:322
  31.5 1.6 %copy.16 = bf16[128,512]{1,0:T(8,128)(2,1)} copy(bf16[128,512]{1,0:T(8,128)(2,1)} %shard_map.136) | data formatting | bytes 262144
